TPU v7x, 512 devices: a whole 4x8x8 slice. The times are simulated.
512 devices in a mesh: section: 8 (over z_hi, core), tensor: 8 (over x, z_lo), dp: 8 (over y).
Axes of the slice: x: 4, y: 8, z: 8 (z_hi: 4, z_lo: 2; z = z_hi * 2 + z_lo), core: 2. Of those that a mesh axis runs over, the one named last changes fastest.
Arguments:
- activations: bfloat16 [8, 16, 64, 4096], P('section', 'dp', None, 'tensor')
- cotangent: bfloat16 [16, 64, 4096], P('dp', None, 'tensor'), may hold values from -6 to 6
- lengths: int32 [16], P('dp'), may hold values from 16 to 64
- weights: bfloat16 [8, 4096, 4096], P('section', 'tensor', 'dp'), may hold values from -0.0625 to 0.0625
- gains: bfloat16 [8, 4096], P('section', 'tensor'), may hold values from 0.25 to 1.75
Outputs:
- input_grads: bfloat16 [8, 16, 64, 4096], P('section', 'dp', None, 'tensor')
- weight_grads: float32 [8, 4096, 4096], P('section', 'tensor', 'dp')
- gain_grads: float32 [8, 4096], P('section', 'tensor')
All inputs are finite; a program needn't handle non-finite values.
Results may differ from a plain program's by a relative error of at most 0.022.
Values may be sent and summed in bfloat16 or wider, within the bound.
A program may use at most 64 MiB of HBM per device.

v0:
```python
import jax
import jax.numpy as jnp
from jax import lax
from jax.sharding import PartitionSpec as P

eps = 1e-05


def passed_along(value, axis, steps):
    count = lax.axis_size(axis)
    first, last = (max(0, -steps), min(count, count - steps))
    return lax.ppermute(value, axis, [(source, source + steps) for source in range(first, last)])


def per_device(activations, cotangent, lengths, weights, gains):
    sections = lax.axis_size("section")
    section_index = lax.axis_index("section")
    shards = lax.axis_size("tensor")
    input_rows = activations[0].astype(jnp.float32)
    micro, seqlen, cols = input_rows.shape
    width = cols * shards
    sums = lax.psum(jnp.sum(input_rows * input_rows, axis=2), "tensor")
    inverse_scale = lax.rsqrt(sums / width + eps)
    norm_gain = gains[0].astype(jnp.float32)
    centered_input = input_rows * inverse_scale[..., None]
    normalized_rows = (centered_input * norm_gain).astype(jnp.bfloat16)
    rows_full = lax.all_gather(weights[0], "dp", axis=1, tiled=True)
    positions = jnp.arange(seqlen, dtype=jnp.int32)
    keep = positions[None, :] < lengths[:, None]
    top = jnp.where(keep[..., None], cotangent, jnp.zeros_like(cotangent))
    stash_init = jnp.zeros((micro, seqlen, width), jnp.bfloat16)
    grads_init = jnp.zeros((micro, seqlen, cols), jnp.bfloat16)
    incoming_init = jnp.zeros((seqlen, cols), jnp.bfloat16)
    gain_init = jnp.zeros((cols,), jnp.float32)

    def advance(step, carry):
        incoming, grads_out, stash, gain_acc = carry
        index = step - (sections - 1 - section_index)
        active = jnp.logical_and(index >= 0, index < micro)
        slot_position = jnp.clip(index, 0, micro - 1)
        own_top = lax.dynamic_index_in_dim(top, slot_position, 0, keepdims=False)
        upstream_grad = jnp.where(section_index == sections - 1, own_top, incoming)
        full = lax.all_gather(upstream_grad, "tensor", axis=1, tiled=True)
        backward_signal = lax.dot_general(
            full, rows_full, (((1,), (1,)), ((), ())), preferred_element_type=jnp.float32
        )
        input_at_slot = lax.dynamic_index_in_dim(centered_input, slot_position, 0, keepdims=False)
        scale_slot = lax.dynamic_index_in_dim(inverse_scale, slot_position, 0, keepdims=False)
        gain_weighted = norm_gain * backward_signal
        row_part = lax.psum(jnp.sum(gain_weighted * input_at_slot, axis=1), "tensor")
        loss_total = upstream_grad.astype(jnp.float32) + scale_slot[:, None] * (
            gain_weighted - input_at_slot * (row_part / width)[:, None]
        )
        sent = loss_total.astype(jnp.bfloat16)
        grads_out = jnp.where(
            active, lax.dynamic_update_index_in_dim(grads_out, sent, slot_position, 0), grads_out
        )
        stash = jnp.where(
            active, lax.dynamic_update_index_in_dim(stash, full, slot_position, 0), stash
        )
        gain_acc = gain_acc + jnp.where(
            active, jnp.sum(backward_signal * input_at_slot, axis=0), jnp.zeros_like(gain_acc)
        )
        incoming = passed_along(sent, "section", -1)
        return (incoming, grads_out, stash, gain_acc)

    final = lax.fori_loop(
        0, sections + micro - 1, advance, (incoming_init, grads_init, stash_init, gain_init)
    )
    grads_out = final[1]
    stash = final[2]
    gain_acc = final[3]
    normed_flat = normalized_rows.reshape(micro * seqlen, cols)
    full_all = stash.reshape(micro * seqlen, width)
    shard_t = lax.psum_scatter(
        lax.dot_general(
            full_all, normed_flat, (((0,), (0,)), ((), ())), preferred_element_type=jnp.float32
        ).astype(jnp.bfloat16),
        "dp",
        scatter_dimension=0,
        tiled=True,
    ).astype(jnp.float32)
    weight_grad = shard_t.T
    gain_grad = lax.psum(gain_acc, "dp")
    return (grads_out[None], weight_grad[None], gain_grad[None])


def solution(mesh):
    in_specs = (
        P("section", "dp", None, "tensor"),
        P("dp", None, "tensor"),
        P("dp"),
        P("section", "tensor", "dp"),
        P("section", "tensor"),
    )
    out_specs = (
        P("section", "dp", None, "tensor"),
        P("section", "tensor", "dp"),
        P("section", "tensor"),
    )
    return jax.shard_map(
        per_device, mesh=mesh, in_specs=in_specs, out_specs=out_specs, check_vma=False
    )
```

profile of v0, /device:TPU:56, one launch (start us, length us, event | category | flops | bytes accessed | tf_op | source)
XLA Modules:
  0.0 633.2 jit_solution(11443693343518285343)
XLA Ops:
  9.7 20.6 %psum.27 = f32[2,64]{1,0:T(2,128)S(1)} all-reduce(f32[2,64]{1,0:T(2,128)S(1)} %fusion.9), channel_id=1, replica_groups=mesh['section'=8,'tensor'=8,'dp'=8] {'tensor'}, use_global_device_ids=true, to_apply=%region_1.0 | all-reduce | flops 128 | bytes 1024 | tf_op jit(solution)/shard_map/psum | solution.py:22
  33.0 36.9 %all-gather.3.cloned.1.call-done = bf16[1,512,4096]{2,1,0:T(8,128)(2,1)} async-done(((bf16[1,512,512]{2,1,0:T(8,128)(2,1)}), bf16[1,512,4096]{2,1,0:T(8,128)(2,1)}) %all-gather.3.cloned.1.call-update) | async-done | bytes 4194320 | tf_op jit(solution)/shard_map/all_gather | solution.py:27
  70.0 489.8 %while.22 = (s32[]{:T(128)}, bf16[64,512]{1,0:T(8,128)(2,1)S(1)}, bf16[2,64,512]{2,1,0:T(8,128)(2,1)S(1)}, bf16[2,64,4096]{2,1,0:T(8,128)(2,1)S(1)}, f32[512]{0:...) while((s32[]{:T(128)}, bf16[64,512]{1,0:T(8,128)(2,1)S(1)}, ...), condition=%wide.region_6.7_spmd.clone, body=%wide.region_2.6_spmd.clone.sunk | while | flops 269157440 | bytes 8141840 | solution.py:67
  70.1 30.0 %all_gather.15 = bf16[64,4096]{1,0:T(8,128)(2,1)S(1)} all-gather(bf16[64,512]{1,0:T(8,128)(2,1)S(1)} %bitcast_select_fusion.4), channel_id=1, replica_groups=mesh['section'=8,'tensor'=8,'dp'=8] {'tensor'}, dimensions={1}, use_global_device_ids=true | all-gather | bytes 589824 | tf_op jit(solution)/shard_map/while/body/eval_jaxpr/all_gather | solution.py:43
  100.1 3.7 fusion.23
  103.8 20.0 %psum.31 = f32[64]{0:T(128)S(1)} all-reduce(f32[64]{0:T(128)S(1)} %get-tuple-element.416), channel_id=1, replica_groups=mesh['section'=8,'tensor'=8,'dp'=8] {'tensor'}, use_global_device_ids=true, to_apply=%region_4.4 | all-reduce | flops 64 | bytes 512 | tf_op jit(solution)/shard_map/while/body/eval_jaxpr/psum | solution.py:50
  123.9 1.3 collective-permute-start
  125.3 1.7 collective-permute-done
  127.0 30.1 %all_gather.15 = bf16[64,4096]{1,0:T(8,128)(2,1)S(1)} all-gather(bf16[64,512]{1,0:T(8,128)(2,1)S(1)} %bitcast_select_fusion.4), channel_id=1, replica_groups=mesh['section'=8,'tensor'=8,'dp'=8] {'tensor'}, dimensions={1}, use_global_device_ids=true | all-gather | bytes 589824 | tf_op jit(solution)/shard_map/while/body/eval_jaxpr/all_gather | solution.py:43
  157.1 3.7 fusion.23
  160.8 16.3 %psum.31 = f32[64]{0:T(128)S(1)} all-reduce(f32[64]{0:T(128)S(1)} %get-tuple-element.416), channel_id=1, replica_groups=mesh['section'=8,'tensor'=8,'dp'=8] {'tensor'}, use_global_device_ids=true, to_apply=%region_4.4 | all-reduce | flops 64 | bytes 512 | tf_op jit(solution)/shard_map/while/body/eval_jaxpr/psum | solution.py:50
  177.2 1.3 collective-permute-start
  178.7 1.7 collective-permute-done
  180.4 30.2 %all_gather.15 = bf16[64,4096]{1,0:T(8,128)(2,1)S(1)} all-gather(bf16[64,512]{1,0:T(8,128)(2,1)S(1)} %bitcast_select_fusion.4), channel_id=1, replica_groups=mesh['section'=8,'tensor'=8,'dp'=8] {'tensor'}, dimensions={1}, use_global_device_ids=true | all-gather | bytes 589824 | tf_op jit(solution)/shard_map/while/body/eval_jaxpr/all_gather | solution.py:43
  210.6 3.7 fusion.23
  214.3 17.7 %psum.31 = f32[64]{0:T(128)S(1)} all-reduce(f32[64]{0:T(128)S(1)} %get-tuple-element.416), channel_id=1, replica_groups=mesh['section'=8,'tensor'=8,'dp'=8] {'tensor'}, use_global_device_ids=true, to_apply=%region_4.4 | all-reduce | flops 64 | bytes 512 | tf_op jit(solution)/shard_map/while/body/eval_jaxpr/psum | solution.py:50
  232.0 1.3 collective-permute-start
  233.5 1.7 collective-permute-done
  235.2 29.6 %all_gather.15 = bf16[64,4096]{1,0:T(8,128)(2,1)S(1)} all-gather(bf16[64,512]{1,0:T(8,128)(2,1)S(1)} %bitcast_select_fusion.4), channel_id=1, replica_groups=mesh['section'=8,'tensor'=8,'dp'=8] {'tensor'}, dimensions={1}, use_global_device_ids=true | all-gather | bytes 589824 | tf_op jit(solution)/shard_map/while/body/eval_jaxpr/all_gather | solution.py:43
  264.8 3.7 fusion.23
  268.5 17.0 %psum.31 = f32[64]{0:T(128)S(1)} all-reduce(f32[64]{0:T(128)S(1)} %get-tuple-element.416), channel_id=1, replica_groups=mesh['section'=8,'tensor'=8,'dp'=8] {'tensor'}, use_global_device_ids=true, to_apply=%region_4.4 | all-reduce | flops 64 | bytes 512 | tf_op jit(solution)/shard_map/while/body/eval_jaxpr/psum | solution.py:50
  285.7 1.3 collective-permute-start
  287.2 1.7 collective-permute-done
  288.8 30.0 %all_gather.15 = bf16[64,4096]{1,0:T(8,128)(2,1)S(1)} all-gather(bf16[64,512]{1,0:T(8,128)(2,1)S(1)} %bitcast_select_fusion.4), channel_id=1, replica_groups=mesh['section'=8,'tensor'=8,'dp'=8] {'tensor'}, dimensions={1}, use_global_device_ids=true | all-gather | bytes 589824 | tf_op jit(solution)/shard_map/while/body/eval_jaxpr/all_gather | solution.py:43
  318.9 3.7 fusion.23
  322.6 17.3 %psum.31 = f32[64]{0:T(128)S(1)} all-reduce(f32[64]{0:T(128)S(1)} %get-tuple-element.416), channel_id=1, replica_groups=mesh['section'=8,'tensor'=8,'dp'=8] {'tensor'}, use_global_device_ids=true, to_apply=%region_4.4 | all-reduce | flops 64 | bytes 512 | tf_op jit(solution)/shard_map/while/body/eval_jaxpr/psum | solution.py:50
  340.0 1.3 collective-permute-start
  341.5 1.7 collective-permute-done
  343.2 29.9 %all_gather.15 = bf16[64,4096]{1,0:T(8,128)(2,1)S(1)} all-gather(bf16[64,512]{1,0:T(8,128)(2,1)S(1)} %bitcast_select_fusion.4), channel_id=1, replica_groups=mesh['section'=8,'tensor'=8,'dp'=8] {'tensor'}, dimensions={1}, use_global_device_ids=true | all-gather | bytes 589824 | tf_op jit(solution)/shard_map/while/body/eval_jaxpr/all_gather | solution.py:43
  373.0 3.7 fusion.23
  376.7 17.0 %psum.31 = f32[64]{0:T(128)S(1)} all-reduce(f32[64]{0:T(128)S(1)} %get-tuple-element.416), channel_id=1, replica_groups=mesh['section'=8,'tensor'=8,'dp'=8] {'tensor'}, use_global_device_ids=true, to_apply=%region_4.4 | all-reduce | flops 64 | bytes 512 | tf_op jit(solution)/shard_map/while/body/eval_jaxpr/psum | solution.py:50
  395.3 1.7 collective-permute-done
  397.0 30.3 %all_gather.15 = bf16[64,4096]{1,0:T(8,128)(2,1)S(1)} all-gather(bf16[64,512]{1,0:T(8,128)(2,1)S(1)} %bitcast_select_fusion.4), channel_id=1, replica_groups=mesh['section'=8,'tensor'=8,'dp'=8] {'tensor'}, dimensions={1}, use_global_device_ids=true | all-gather | bytes 589824 | tf_op jit(solution)/shard_map/while/body/eval_jaxpr/all_gather | solution.py:43
  427.3 3.7 fusion.23
  431.0 16.8 %psum.31 = f32[64]{0:T(128)S(1)} all-reduce(f32[64]{0:T(128)S(1)} %get-tuple-element.416), channel_id=1, replica_groups=mesh['section'=8,'tensor'=8,'dp'=8] {'tensor'}, use_global_device_ids=true, to_apply=%region_4.4 | all-reduce | flops 64 | bytes 512 | tf_op jit(solution)/shard_map/while/body/eval_jaxpr/psum | solution.py:50
  449.4 1.7 collective-permute-done
  451.1 30.5 %all_gather.15 = bf16[64,4096]{1,0:T(8,128)(2,1)S(1)} all-gather(bf16[64,512]{1,0:T(8,128)(2,1)S(1)} %bitcast_select_fusion.4), channel_id=1, replica_groups=mesh['section'=8,'tensor'=8,'dp'=8] {'tensor'}, dimensions={1}, use_global_device_ids=true | all-gather | bytes 589824 | tf_op jit(solution)/shard_map/while/body/eval_jaxpr/all_gather | solution.py:43
  481.7 3.7 fusion.23
  485.4 16.5 %psum.31 = f32[64]{0:T(128)S(1)} all-reduce(f32[64]{0:T(128)S(1)} %get-tuple-element.416), channel_id=1, replica_groups=mesh['section'=8,'tensor'=8,'dp'=8] {'tensor'}, use_global_device_ids=true, to_apply=%region_4.4 | all-reduce | flops 64 | bytes 512 | tf_op jit(solution)/shard_map/while/body/eval_jaxpr/psum | solution.py:50
  503.5 1.7 collective-permute-done
  505.2 30.1 %all_gather.15 = bf16[64,4096]{1,0:T(8,128)(2,1)S(1)} all-gather(bf16[64,512]{1,0:T(8,128)(2,1)S(1)} %bitcast_select_fusion.4), channel_id=1, replica_groups=mesh['section'=8,'tensor'=8,'dp'=8] {'tensor'}, dimensions={1}, use_global_device_ids=true | all-gather | bytes 589824 | tf_op jit(solution)/shard_map/while/body/eval_jaxpr/all_gather | solution.py:43
  535.3 3.7 fusion.23
  539.0 17.6 %psum.31 = f32[64]{0:T(128)S(1)} all-reduce(f32[64]{0:T(128)S(1)} %get-tuple-element.416), channel_id=1, replica_groups=mesh['section'=8,'tensor'=8,'dp'=8] {'tensor'}, use_global_device_ids=true, to_apply=%region_4.4 | all-reduce | flops 64 | bytes 512 | tf_op jit(solution)/shard_map/while/body/eval_jaxpr/psum | solution.py:50
  558.2 1.7 collective-permute-done
  559.9 3.2 bitcast_convert_fusion
  563.1 15.6 %psum.28 = f32[1,512]{1,0:T(1,128)} all-reduce(f32[1,512]{1,0:T(1,128)S(1)} %bitcast.66), channel_id=1, replica_groups=mesh['section'=8,'tensor'=8,'dp'=8] {'dp'}, use_global_device_ids=true, to_apply=%region_8.9 | all-reduce | flops 512 | bytes 4096 | tf_op jit(solution)/shard_map/psum | solution.py:84
  578.8 45.1 %reduce-scatter.2.cloned.1.call-done = bf16[512,512]{1,0:T(8,128)(2,1)} async-done(((bf16[4096,512]{1,0:T(8,128)(2,1)}), bf16[512,512]{1,0:T(8,128)(2,1)}) %reduce-scatter.2.cloned.1.call-update) | async-done | bytes 524304 | tf_op jit(solution)/shard_map/reduce_scatter | solution.py:75
  625.1 1.3 copy.8
  (77 shorter events, 14.4 us)
Async XLA Ops:
  7.2 62.7 %all-gather.3.cloned.1.call-start = ((), (), s32[]{:S(2)}) async-start(), calls=%async_computation.2 | async-start | bytes 4718592 | tf_op jit(solution)/shard_map/all_gather | solution.py:27
  7.9 616.0 %reduce-scatter.2.cloned.1.call-start = ((), (), s32[]{:S(2)}) async-start(), calls=%async_computation.1 | async-start | bytes 4718592 | tf_op jit(solution)/shard_map/reduce_scatter | solution.py:75
  70.0 489.9 %copy-start.1 = (bf16[1,2,64,512]{3,2,1,0:T(8,128)(2,1)S(1)}, bf16[1,2,64,512]{3,2,1,0:T(8,128)(2,1)}, u32[]{:S(2)}) copy-start(bf16[1,2,64,512]{3,2,1,0:T(8,128)(2,1)} %param.7) | copy-start | bytes 393220
  123.9 3.1 collective-permute-start
  177.2 3.1 collective-permute-start
  232.0 3.1 collective-permute-start
  285.7 3.1 collective-permute-start
  340.0 3.1 collective-permute-start
  393.8 3.1 collective-permute-start
  447.9 3.1 collective-permute-start
  502.0 3.1 collective-permute-start
  556.7 3.1 collective-permute-start
  559.9 3.3 copy-start
Sparse Core Ops, SparseCore 0:
  10.1 59.7 all-gather.2
  563.3 60.5 reduce-scatter.1
where the time goes:
time: 637 us; the launch traced here: 633 us
  blocking collectives  463 us (73%)
  waiting for transfers between devices  97.6 us (15%)
  matrix products  36.5 us (6%)
  between operations  14.1 us (2%)
  starting transfers between devices  11.7 us (2%)
  other arithmetic  8.29 us (1%)
    all_gather x9, blocking collectives, advance(): full = lax.all_gather(upstream_grad, 'tensor', axis=1, tiled=True)  271 us
    psum x9, blocking collectives, advance(): lax.psum(jnp.sum(gain_weighted * input_at_slot, axis=1), 'tensor')  156 us
    reduce_scatter x1, waiting for transfers between devices, per_device(): lax.psum_scatter(lax.dot_general(full_all, normed_flat, (((0,), (0,)), ((...  45.1 us
    all_gather x1, waiting for transfers between devices, per_device(): rows_full = lax.all_gather(weights[0], 'dp', axis=1, tiled=True)  36.9 us
    dot_general x9, matrix products, advance(): lax.dot_general(full, rows_full, (((1,), (1,)), ((), ())), preferred_elem...  33.3 us
    psum x1, blocking collectives, per_device(): sums = lax.psum(jnp.sum(input_rows * input_rows, axis=2), 'tensor')  20.6 us
    psum x1, blocking collectives, per_device(): gain_grad = lax.psum(gain_acc, 'dp')  15.6 us
    ppermute x9, waiting for transfers between devices, passed_along(): lax.ppermute(value, axis, [(source, source + steps) for source in range(f...  14.9 us
  transfers between devices with their start and end apart: 11, of which 11 were waited for; matrix products, arithmetic and copies ran while one was open for 1% of the time, Pallas kernels for 0%

commit v1 on v0

v1 whole, which is shorter than its diff:
```python
import functools

import jax
import jax.numpy as jnp
from jax import lax
from jax.experimental import pallas as pl
from jax.experimental.pallas import tpu as pltpu
from jax.sharding import PartitionSpec as P

EPS = 1e-05
LANES = 128
CHUNKS = 4
PIECES = 4
MESH = pl.DeviceIdType.MESH


def remote(src, dst, send, recv, dev):
    return pltpu.make_async_remote_copy(
        src_ref=src, dst_ref=dst, send_sem=send, recv_sem=recv, device_id=dev, device_id_type=MESH
    )


def wide(tile, cols):
    return jnp.concatenate([tile] * (cols // LANES), axis=1)


def kernel(
    sizes,
    lengths_ref, x_ref, cot_ref, w_ref, gain_ref,
    grads_out, wgrad_out, gain_out,
    w_all, inbox, grad_all, corr, corr_own, normed_all, swapped, xhat, upd, outbox,
    squares, rterm, gain_part,
    w_send, w_recv, relay_send, relay_recv, swap_send, swap_recv,
    sq_send, sq_recv, corr_send, corr_recv, norm_send, norm_recv,
    r_send, r_recv, gn_send, gn_recv,
):
    ns, nt, nd = sizes
    s, t, d = lax.axis_index("section"), lax.axis_index("tensor"), lax.axis_index("dp")
    tokens, cols = x_ref.shape
    width = cols * nt
    rows = tokens // CHUNKS
    seqlen = tokens // 2
    first, last = s == ns - 1, s == 0
    dp_peer = lambda k: lax.rem(d + k, nd)
    t_peer = lambda k: lax.rem(t + k, nt)

    barrier = pltpu.get_barrier_semaphore()
    for k in range(1, nd):
        pl.semaphore_signal(barrier, 1, device_id={"dp": dp_peer(k)}, device_id_type=MESH)
    for k in range(1, nt):
        pl.semaphore_signal(barrier, 1, device_id={"tensor": t_peer(k)}, device_id_type=MESH)

    @pl.when(jnp.logical_not(last))
    def _():
        for k in range(nt):
            pl.semaphore_signal(
                barrier, 1, device_id={"section": s - 1, "tensor": t_peer(k)}, device_id_type=MESH
            )

    @pl.when(jnp.logical_not(first))
    def _():
        for k in range(nt):
            pl.semaphore_signal(
                barrier, 1, device_id={"section": s + 1, "tensor": t_peer(k)}, device_id_type=MESH
            )

    w_all[d] = w_ref[...].T
    x = x_ref[...].astype(jnp.float32)
    squares[t] = jnp.broadcast_to(jnp.sum(x * x, axis=1, keepdims=True), (tokens, LANES))

    @pl.when(first)
    def _():
        position = lax.broadcasted_iota(jnp.int32, (seqlen, cols), 0)
        for m in range(2):
            part = slice(m * seqlen, (m + 1) * seqlen)
            masked = jnp.where(
                position < lengths_ref[m], cot_ref[part, :].astype(jnp.float32), 0.0
            ).astype(jnp.bfloat16)
            outbox[part, :cols] = masked
            inbox[t, part, :cols] = masked
        outbox[:, cols:] = jnp.zeros((tokens, LANES), jnp.bfloat16)
        inbox[t, :, cols:] = jnp.zeros((tokens, LANES), jnp.bfloat16)
        corr[...] = jnp.zeros_like(corr)

    expected = nd - 1 + nt - 1 + nt * (
        jnp.where(last, 0, 1) + jnp.where(first, 0, 1)
    )
    pl.semaphore_wait(barrier, expected)

    size = cols // PIECES

    def w_copy(hop, piece, way):
        block = lax.rem(d - way * (hop - 1) + 2 * nd, nd)
        view = w_all.at[block, pl.ds(piece * size, size)]
        side = 0 if way > 0 else 1
        return remote(
            view, view, w_send.at[side, hop - 1, piece], w_recv.at[side, hop - 1, piece],
            {"dp": lax.rem(d + way + nd, nd)},
        )

    def w_arrived(hop, piece, way):
        block = lax.rem(d - way * hop + 2 * nd, nd)
        view = w_all.at[block, pl.ds(piece * size, size)]
        side = 0 if way > 0 else 1
        remote(
            view, view, w_send.at[side, hop - 1, piece], w_recv.at[side, hop - 1, piece],
            {"dp": lax.rem(d + way + nd, nd)},
        ).wait_recv()

    half = PIECES // 2
    hops = nd // 2
    travels = lambda hop, piece, way: hop < hops or (piece < half) == (way > 0)

    def w_hop(hop):
        for piece in range(PIECES):
            for way in (1, -1):
                if travels(hop, piece, way):
                    if hop > 1:
                        w_arrived(hop - 1, piece, way)
                    w_copy(hop, piece, way).start()

    w_hop(1)

    def sq_copy(k, src):
        return remote(
            squares.at[src], squares.at[src], sq_send.at[k], sq_recv.at[src], {"tensor": t_peer(k)}
        )

    for k in range(1, nt):
        sq_copy(k, t).start()

    def first_copy(c, k):
        view = pl.ds(c * rows, rows)
        return remote(
            outbox.at[view], inbox.at[t, view], relay_send.at[c, k], relay_recv.at[c, t],
            {"tensor": t_peer(k)},
        )

    def relay_copy(c, k):
        view = pl.ds(c * rows, rows)
        return remote(
            outbox.at[view], inbox.at[t, view], relay_send.at[c, k], relay_recv.at[c, t],
            {"section": s - 1, "tensor": t_peer(k)},
        )

    @pl.when(first)
    def _():
        for c in range(CHUNKS):
            for k in range(1, nt):
                first_copy(c, k).start()

    for k in range(1, nt):
        sq_copy(k, t_peer(k)).wait_recv()
    total = squares[0]
    for j in range(1, nt):
        total = total + squares[j]
    scale = wide(lax.rsqrt(total / width + EPS), cols)
    gain = gain_ref[...].astype(jnp.float32)
    x = x_ref[...].astype(jnp.float32) * scale
    xhat[...] = x
    normed_all[d] = (x * gain).astype(jnp.bfloat16)
    corr_own[...] = (x * scale).astype(jnp.bfloat16)
    upd[...] = scale

    def corr_copy(k):
        return remote(
            corr_own, corr.at[t], corr_send.at[k], corr_recv.at[t],
            {"section": s - 1, "tensor": t_peer(k)},
        )

    @pl.when(jnp.logical_not(last))
    def _():
        for k in range(nt):
            corr_copy(k).start()

    for hop in range(2, hops + 1):
        w_hop(hop)
    for hop in range(hops - 1, hops + 1):
        for piece in range(PIECES):
            for way in (1, -1):
                if travels(hop, piece, way) and not travels(hop + 1, piece, way) or hop == hops and travels(hop, piece, way):
                    w_arrived(hop, piece, way)

    def norm_copy(k, src):
        return remote(
            normed_all.at[src], normed_all.at[src], norm_send.at[k], norm_recv.at[src],
            {"dp": dp_peer(k)},
        )

    for k in range(1, nd):
        norm_copy(k, d).start()

    @pl.when(jnp.logical_not(first))
    def _():
        for k in range(nt):
            src = t_peer(k)
            remote(
                corr_own, corr.at[src], corr_send.at[k], corr_recv.at[src], {"tensor": t_peer(1)}
            ).wait_recv()

    gain_part[d] = jnp.zeros((8, cols), jnp.float32)

    def relay_arrived(c, k):
        src = t_peer(k)
        view = pl.ds(c * rows, rows)
        remote(
            outbox.at[view], inbox.at[src, view], relay_send.at[c, k], relay_recv.at[c, src],
            {"tensor": t_peer(1)},
        ).wait_recv()

    def swap_copy(c, k):
        view = pl.ds(pl.multiple_of(c * rows, rows), rows)
        return remote(
            grad_all.at[dp_peer(k), view], swapped.at[d, view], swap_send.at[c, k],
            swap_recv.at[c, d], {"dp": dp_peer(k)},
        )

    def swap_arrived(c, k):
        src = dp_peer(k)
        view = pl.ds(pl.multiple_of(c * rows, rows), rows)
        remote(
            grad_all.at[src, view], swapped.at[src, view], swap_send.at[c, k],
            swap_recv.at[c, src], {"dp": dp_peer(1)},
        ).wait_recv()

    def chunk(c, carry):
        view = pl.ds(pl.multiple_of(c * rows, rows), rows)

        @pl.when(jnp.logical_not(first))
        def _():
            relay_arrived(c, 0)

        for k in range(1, nt):
            relay_arrived(c, k)
        r = inbox[0, view, cols:].astype(jnp.float32)
        for j in range(1, nt):
            r = r + inbox[j, view, cols:].astype(jnp.float32)
        r = wide(r, cols)
        back = jnp.zeros((rows, cols), jnp.float32)
        for j in range(nt):
            g = inbox[j, view, :cols].astype(jnp.float32) - corr[j, view].astype(jnp.float32) * r
            g = g.astype(jnp.bfloat16)
            grad_all[j, view] = g
            back = back + jnp.dot(g, w_all[j], preferred_element_type=jnp.float32)
        xh = xhat[view]
        weighted = gain * back
        part = jnp.sum(weighted * xh, axis=1, keepdims=True) * (1.0 / width)
        u = grad_all[t, view].astype(jnp.float32) + upd[view] * weighted
        outbox[view, :cols] = u.astype(jnp.bfloat16)
        tile = jnp.broadcast_to(part, (rows, LANES)).astype(jnp.bfloat16)
        outbox[view, cols:] = tile

        @pl.when(jnp.logical_not(last))
        def _():
            for k in range(nt):
                relay_copy(c, k).start()

        for k in range(1, nd):
            swap_copy(c, k).start()
        swapped[d, view] = grad_all[d, view]
        upd[view] = u
        rterm[t, view] = tile
        gain_part[d] = gain_part[d] + jnp.sum((back * xh).reshape(rows // 8, 8, cols), axis=0)
        return carry

    @pl.when(first)
    def _():
        for c in range(CHUNKS):
            for k in range(1, nt):
                first_copy(c, k).wait_send()

    lax.fori_loop(0, CHUNKS, chunk, 0)

    def r_copy(k, src):
        return remote(rterm.at[src], rterm.at[src], r_send.at[k], r_recv.at[src], {"tensor": t_peer(k)})

    def gn_copy(k, src):
        return remote(
            gain_part.at[src], gain_part.at[src], gn_send.at[k], gn_recv.at[src], {"dp": dp_peer(k)}
        )

    for k in range(1, nt):
        r_copy(k, t).start()
    for k in range(1, nd):
        gn_copy(k, d).start()
    for k in range(1, nt):
        r_copy(k, t_peer(k)).wait_recv()
    r = rterm[0].astype(jnp.float32)
    for j in range(1, nt):
        r = r + rterm[j].astype(jnp.float32)
    grads_out[...] = (
        upd[...] - corr_own[...].astype(jnp.float32) * wide(r, cols)
    ).astype(jnp.bfloat16)
    for k in range(1, nd):
        gn_copy(k, dp_peer(k)).wait_recv()
    sums = gain_part[0]
    for j in range(1, nd):
        sums = sums + gain_part[j]
    gain_out[...] = jnp.sum(sums, axis=0, keepdims=True)

    for k in range(1, nd):
        norm_copy(k, dp_peer(k)).wait_recv()
        for c in range(CHUNKS):
            swap_arrived(c, k)
    acc = jnp.zeros((cols, cols), jnp.float32)
    for j in range(nd):
        acc = acc + lax.dot_general(
            normed_all[j], swapped[j], (((0,), (0,)), ((), ())), preferred_element_type=jnp.float32
        )
    wgrad_out[...] = acc

    for hop in range(1, hops + 1):
        for piece in range(PIECES):
            for way in (1, -1):
                if travels(hop, piece, way):
                    w_copy(hop, piece, way).wait_send()
    for k in range(1, nt):
        sq_copy(k, t).wait_send()
        r_copy(k, t).wait_send()
    for k in range(1, nd):
        norm_copy(k, d).wait_send()
        gn_copy(k, d).wait_send()
        for c in range(CHUNKS):
            swap_copy(c, k).wait_send()

    @pl.when(jnp.logical_not(last))
    def _():
        for k in range(nt):
            corr_copy(k).wait_send()
            for c in range(CHUNKS):
                relay_copy(c, k).wait_send()


def per_device(activations, cotangent, lengths, weights, gains):
    ns, nt, nd = (lax.axis_size(a) for a in ("section", "tensor", "dp"))
    _, micro, seqlen, cols = activations.shape
    tokens = micro * seqlen
    bf16, f32 = jnp.bfloat16, jnp.float32
    vmem = pl.BlockSpec(memory_space=pltpu.VMEM)
    dma = lambda *shape: pltpu.SemaphoreType.DMA(shape)
    grads, wgrad, gain_grad = pl.pallas_call(
        functools.partial(kernel, (ns, nt, nd)),
        out_shape=(
            jax.ShapeDtypeStruct((tokens, cols), bf16),
            jax.ShapeDtypeStruct((cols, cols), f32),
            jax.ShapeDtypeStruct((1, cols), f32),
        ),
        in_specs=[pl.BlockSpec(memory_space=pltpu.SMEM)] + [vmem] * 4,
        out_specs=(vmem, vmem, vmem),
        scratch_shapes=[
            pltpu.VMEM((nd, cols, cols), bf16),
            pltpu.VMEM((nt, tokens, cols + LANES), bf16),
            pltpu.VMEM((nt, tokens, cols), bf16),
            pltpu.VMEM((nt, tokens, cols), bf16),
            pltpu.VMEM((tokens, cols), bf16),
            pltpu.VMEM((nd, tokens, cols), bf16),
            pltpu.VMEM((nd, tokens, cols), bf16),
            pltpu.VMEM((tokens, cols), f32),
            pltpu.VMEM((tokens, cols), f32),
            pltpu.VMEM((tokens, cols + LANES), bf16),
            pltpu.VMEM((nt, tokens, LANES), f32),
            pltpu.VMEM((nt, tokens, LANES), bf16),
            pltpu.VMEM((nd, 8, cols), f32),
            dma(2, nd // 2, PIECES), dma(2, nd // 2, PIECES),
            dma(CHUNKS, nt), dma(CHUNKS, nt),
            dma(CHUNKS, nd), dma(CHUNKS, nd),
            dma(nt), dma(nt), dma(nt), dma(nt), dma(nd), dma(nd),
            dma(nt), dma(nt), dma(nd), dma(nd),
        ],
        compiler_params=pltpu.CompilerParams(
            collective_id=0, has_side_effects=True, vmem_limit_bytes=48 << 20
        ),
        name="relay",
    )(
        lengths,
        activations.reshape(tokens, cols),
        cotangent.reshape(tokens, cols),
        weights.reshape(cols, cols),
        gains,
    )
    return (
        grads.reshape(1, micro, seqlen, cols),
        wgrad.reshape(1, cols, cols),
        gain_grad,
    )


def solution(mesh):
    in_specs = (
        P("section", "dp", None, "tensor"),
        P("dp", None, "tensor"),
        P("dp"),
        P("section", "tensor", "dp"),
        P("section", "tensor"),
    )
    out_specs = (
        P("section", "dp", None, "tensor"),
        P("section", "tensor", "dp"),
        P("section", "tensor"),
    )
    return jax.shard_map(
        per_device, mesh=mesh, in_specs=in_specs, out_specs=out_specs, check_vma=False
    )
```

time: 637 us -> 174 us (0.27)
  blocking collectives: 463 us -> 0 us
  Pallas kernels: 0 us -> 166 us
  waiting for transfers between devices: 97.6 us -> 0 us
  matrix products: 36.5 us -> 0 us
  between operations: 14.1 us -> 0.66 us
  starting transfers between devices: 11.7 us -> 0 us
  other arithmetic: 8.29 us -> 0 us
    all_gather x9 -> x0, blocking collectives: 271 us -> none  [advance(): full = lax.all_gather(upstream_grad, 'tensor', axis=1, tiled=True)]
    psum x11 -> x0, blocking collectives: 192 us -> none  [the longest x9 156 us: advance(): lax.psum(jnp.sum(gain_weighted * input_at_slot, axis=1), 'tensor')]
    pallas_call x0 -> x1, Pallas kernels: none -> 166 us  [per_device(): pl.pallas_call(functools.partial(kernel, (ns, nt, nd)), out_shape=(jax.Sh...]
    reduce_scatter x1 -> x0, waiting for transfers between devices: 45.1 us -> none  [per_device(): lax.psum_scatter(lax.dot_general(full_all, normed_flat, (((0,), (0,)), ((...]
    all_gather x1 -> x0, waiting for transfers between devices: 36.9 us -> none  [per_device(): rows_full = lax.all_gather(weights[0], 'dp', axis=1, tiled=True)]
    dot_general x10 -> x0, matrix products: 36.5 us -> none  [the longest x9 33.3 us: advance(): lax.dot_general(full, rows_full, (((1,), (1,)), ((), ())), preferred_elem...]
    ppermute x9 -> x0, waiting for transfers between devices: 14.9 us -> none  [passed_along(): lax.ppermute(value, axis, [(source, source + steps) for source in range(f...]
    ppermute x9 -> x0, starting transfers between devices: 11.6 us -> none  [passed_along(): lax.ppermute(value, axis, [(source, source + steps) for source in range(f...]
  transfers between devices with their start and end apart: 11 -> 0, of which waited for: 11 -> 0; matrix products, arithmetic and copies ran while one was open for 1% -> 0% of each run, Pallas kernels for 0% -> 0%
where the time goes in v1:
time: 174 us; the launch traced here: 172 us
  Pallas kernels  166 us (95%)
  local copies, waits for them, and re-layouts  5.72 us (3%)
    pallas_call x1, Pallas kernels, per_device(): pl.pallas_call(functools.partial(kernel, (ns, nt, nd)), out_shape=(jax.Sh...  166 us
    unnamed x13, local copies, waits for them, and re-layouts  5.72 us

profile of v1, /device:TPU:56, one launch (start us, length us, event | category | flops | bytes accessed | tf_op | source)
XLA Modules:
  0.0 172.3 jit_solution(5382047838764350627)
XLA Ops:
  0.6 0.0 copy-start.3
  0.6 0.0 copy-start.4
  0.7 0.7 copy-done.3
  1.3 0.0 copy-done.4
  1.3 0.0 copy-start
  1.3 1.0 copy-done
  2.4 0.0 copy-start.1
  2.4 0.9 copy-done.1
  3.3 0.0 copy-start.2
  3.3 0.9 copy-done.2
  4.2 165.9 %relay.1 = (bf16[128,512]{1,0:T(8,128)(2,1)S(1)}, f32[512,512]{1,0:T(8,128)S(1)}, f32[1,512]{1,0:T(1,128)S(1)}) custom-call(s32[2]{0:T(128)S(1)} %copy-done.4, bf16[128,512]{1,0:T(8,128)(2,1)S(1)} %bitcast.8, bf16[128,512]{1,0:T(8,128)(2,1)S(1)} %bitcast.9, bf16[512,512]{1,0:T(8,128)(2,1)S(1)} %bitcast.6, bf16[1,512]{1,0:T(2,128)(2,1)S(1)} %copy-done.3), custom_call_target="tpu_custom_call" | custom-call | tf_op jit(solution)/shard_map/relay/pallas_call | solution.py:341
  170.1 0.7 copy.11
  170.7 1.0 copy.12
  171.7 0.6 copy.13
Async XLA Ops:
  0.6 0.7 copy-start.3
  0.6 0.7 copy-start.4
  1.3 1.0 copy-start
  2.4 0.9 copy-start.1
  3.3 0.9 copy-start.2

commit v2 on v1

v2 whole, which is shorter than its diff:
```python
import functools

import jax
import jax.numpy as jnp
from jax import lax
from jax.experimental import pallas as pl
from jax.experimental.pallas import tpu as pltpu
from jax.sharding import PartitionSpec as P

EPS = 1e-05
LANES = 128
CHUNKS = 4
WINDOW = 2
Q_PIECES = 2
TURN = 8
FINAL = 1
AHEAD = 2
PIECES = 4
MESH = pl.DeviceIdType.MESH


def remote(src, dst, send, recv, dev):
    return pltpu.make_async_remote_copy(
        src_ref=src, dst_ref=dst, send_sem=send, recv_sem=recv, device_id=dev, device_id_type=MESH
    )


def wide(tile, cols):
    return jnp.concatenate([tile] * (cols // LANES), axis=1)


class Ring:
    def __init__(self, buf, send, recv, d, nd, pieces, window):
        self.buf, self.send, self.recv = buf, send, recv
        self.d, self.nd, self.pieces, self.window = d, nd, pieces, window
        self.hops = nd // 2
        self.size = buf.shape[1] // pieces
        half = pieces // 2
        whole = [(hop, piece) for hop in range(1, self.hops) for piece in range(pieces)]
        self.order = {
            1: whole + [(self.hops, piece) for piece in range(half)],
            -1: whole + [(self.hops, piece) for piece in range(half, pieces)],
        }
        self.steps = len(self.order[1])

    def copy(self, block_hop, hop, piece, way):
        block = lax.rem(self.d - way * block_hop + 2 * self.nd, self.nd)
        view = self.buf.at[block, pl.ds(piece * self.size, self.size)]
        side = 0 if way > 0 else 1
        return remote(
            view, view, self.send.at[side, hop - 1, piece], self.recv.at[side, hop - 1, piece],
            {"dp": lax.rem(self.d + way + self.nd, self.nd)},
        )

    def left(self, i, way):
        hop, piece = self.order[way][i]
        self.copy(hop - 1, hop, piece, way).wait_send()

    def start(self, begin, end):
        for i in range(begin, end):
            for way in (1, -1):
                hop, piece = self.order[way][i]
                if hop > 1:
                    self.copy(hop - 1, hop - 1, piece, way).wait_recv()
                if i >= self.window:
                    self.left(i - self.window, way)
                self.copy(hop - 1, hop, piece, way).start()

    def finish(self):
        for way in (1, -1):
            for hop, piece in self.order[way]:
                if (hop + 1, piece) not in self.order[way]:
                    self.copy(hop, hop, piece, way).wait_recv()

    def drain(self):
        for i in range(max(self.steps - self.window, 0), self.steps):
            for way in (1, -1):
                self.left(i, way)


def kernel(
    sizes,
    lengths_ref, x_hbm, cot_hbm, w_hbm, gain_hbm,
    grads_out, wgrad_out, gain_out,
    x_ref, cot_ref, w_ref, gain_ref,
    w_all, inbox, grad_all, corr, corr_own, normed_all, swapped, xhat, upd, outbox,
    squares, rterm, gain_part, w_part, g_part, back_part, back_sent, back_in, back_now,
    in_sem, w_send, w_recv, q_send, q_recv, relay_send, relay_recv, swap_send, swap_recv,
    sq_send, sq_recv, corr_send, corr_recv, norm_send, norm_recv,
    r_send, r_recv, gn_send, gn_recv, quarter_send, quarter_recv, gq_send, gq_recv,
    back_send, back_recv, spread_send, cs_send, cross_send, cross_recv, turn, free,
):
    ns, nt, nd = sizes
    s, t, d = lax.axis_index("section"), lax.axis_index("tensor"), lax.axis_index("dp")
    tokens, cols = x_ref.shape
    width = cols * nt
    rows = tokens // CHUNKS
    seqlen = tokens // 2
    planes = ns // 2
    part_rows = cols // planes
    plane = s // 2
    first, last = s == ns - 1, s == 0
    odd = lax.rem(s, 2) == 1
    even = jnp.logical_not(odd)
    not_first, not_last = jnp.logical_not(first), jnp.logical_not(last)
    odd_inner = jnp.logical_and(odd, not_first)
    even_inner = jnp.logical_and(even, not_last)
    odd_late = jnp.logical_and(odd, s >= ns // 2)
    hurried = s == ns - 3
    final = s < FINAL
    not_final = jnp.logical_not(final)
    early = jnp.logical_not(odd_late)
    dp_peer = lambda k: lax.rem(d + k, nd)
    t_peer = lambda k: lax.rem(t + k, nt)

    loads = [
        pltpu.make_async_copy(src, dst, in_sem.at[n])
        for n, (src, dst) in enumerate(
            ((w_hbm, w_ref), (x_hbm, x_ref), (cot_hbm, cot_ref), (gain_hbm, gain_ref))
        )
    ]
    for load in loads:
        load.start()

    barrier = pltpu.get_barrier_semaphore()

    def greet(**where):
        pl.semaphore_signal(barrier, 1, device_id=where, device_id_type=MESH)

    for k in range(1, nd):
        greet(dp=dp_peer(k))
    for k in range(1, nt):
        greet(tensor=t_peer(k))

    @pl.when(not_last)
    def _():
        for k in range(nt):
            greet(section=s - 1, tensor=t_peer(k))

    @pl.when(not_first)
    def _():
        for k in range(nt):
            greet(section=s + 1, tensor=t_peer(k))

    @pl.when(odd_inner)
    def _():
        greet(section=ns - 1)

    @pl.when(first)
    def _():
        for p in range(planes - 1):
            greet(section=2 * p + 1)

    loads[0].wait()
    w_all[d] = w_ref[...].T
    loads[2].wait()

    def mask(m):
        def apply(value):
            position = lax.broadcasted_iota(jnp.int32, value.shape, 0)
            kept = jnp.where(position < lengths_ref[m], value.astype(jnp.float32), 0.0)
            return kept.astype(jnp.bfloat16)

        return apply

    @pl.when(odd)
    def _():
        mine = pl.ds(pl.multiple_of(plane * part_rows, part_rows), part_rows)
        for m in range(2):
            part = slice(m * seqlen, (m + 1) * seqlen)
            g_part[t, part] = mask(m)(cot_ref[part, mine])

    @pl.when(first)
    def _():
        w_part[d] = w_all[d, (planes - 1) * part_rows :]
        for m in range(2):
            part = slice(m * seqlen, (m + 1) * seqlen)
            inbox[t, part, :cols] = mask(m)(cot_ref[part])
        inbox[t, :, cols:] = jnp.zeros((tokens, LANES), jnp.bfloat16)

    loads[1].wait()
    loads[3].wait()
    x = x_ref[...].astype(jnp.float32)
    squares[t] = jnp.broadcast_to(jnp.sum(x * x, axis=1, keepdims=True), (tokens, LANES))

    expected = (
        nd - 1 + nt - 1
        + nt * (jnp.where(last, 0, 1) + jnp.where(first, 0, 1))
        + jnp.where(odd_inner, 1, 0) + jnp.where(first, planes - 1, 0)
    )
    pl.semaphore_wait(barrier, expected)

    whole = Ring(w_all, w_send, w_recv, d, nd, PIECES, WINDOW)
    quarter = Ring(w_part, q_send, q_recv, d, nd, Q_PIECES, 99)

    def quarter_copy(p):
        return remote(
            w_all.at[d, pl.ds(p * part_rows, part_rows)], w_part.at[d],
            quarter_send.at[p], quarter_recv, {"section": 2 * p + 1},
        )

    def gq_copy(k, src):
        return remote(
            g_part.at[src], g_part.at[src], gq_send.at[k], gq_recv.at[src], {"tensor": t_peer(k)}
        )

    def sq_copy(k, src):
        return remote(
            squares.at[src], squares.at[src], sq_send.at[k], sq_recv.at[src], {"tensor": t_peer(k)}
        )

    def spread_copy(c, k, src):
        view = pl.ds(pl.multiple_of(c * rows, rows), rows)
        return remote(
            inbox.at[src, view], inbox.at[src, view], spread_send.at[c, k], relay_recv.at[c, src],
            {"tensor": t_peer(k)},
        )

    def relay_copy(c, k, near):
        view = pl.ds(pl.multiple_of(c * rows, rows), rows)
        where = {"section": s - 1, "tensor": t_peer(k)} if near else {"section": s - 1}
        return remote(
            outbox.at[view], inbox.at[t, view], relay_send.at[c, k], relay_recv.at[c, t], where
        )

    def back_copy(c, p):
        view = pl.ds(c * rows, rows)
        return remote(
            back_sent.at[view], back_in.at[p, view], back_send.at[c], back_recv.at[c, p],
            {"section": ns - 1},
        )

    def corr_copy(k, near):
        where = {"section": s - 1, "tensor": t_peer(k)} if near else {"section": s - 1}
        return remote(corr_own, corr.at[t], corr_send.at[k], corr_recv.at[t], where)

    def corr_spread(k, src):
        return remote(
            corr.at[src], corr.at[src], cs_send.at[k], corr_recv.at[src], {"tensor": t_peer(k)}
        )

    def norm_copy(k, src):
        return remote(
            normed_all.at[src], normed_all.at[src], norm_send.at[k], norm_recv.at[src],
            {"dp": dp_peer(k)},
        )

    def swap_copy(c, k):
        view = pl.ds(pl.multiple_of(c * rows, rows), rows)
        return remote(
            grad_all.at[dp_peer(k), view], swapped.at[d, view], swap_send.at[c, k],
            swap_recv.at[c, d], {"dp": dp_peer(k)},
        )

    def slice_of(c):
        groups = cols // LANES
        height = rows // (nt // groups)
        mine = pl.ds(pl.multiple_of(c * rows + t // groups * height, height), height)
        return mine, pl.ds(pl.multiple_of(lax.rem(t, groups) * LANES, LANES), LANES)

    def slice_copy(c, k):
        mine, lanes = slice_of(c)
        return remote(
            grad_all.at[dp_peer(k), mine, lanes], swapped.at[d, mine, lanes], swap_send.at[c, k],
            swap_recv.at[c, d], {"dp": dp_peer(k)},
        )

    def cross_copy(c, k):
        mine, lanes = slice_of(c)
        view = swapped.at[:, mine, lanes]
        return remote(
            view, view, cross_send.at[c, k], cross_recv.at[c, t], {"tensor": t_peer(k)}
        )

    @pl.when(first)
    def _():
        for p in range(planes - 1):
            quarter_copy(p).start()

    @pl.when(hurried)
    def _():
        whole.start(0, PIECES // 2)

    @pl.when(s == ns - 2)
    def _():
        whole.start(0, PIECES)

    @pl.when(odd)
    def _():
        for k in range(1, nt):
            gq_copy(k, t).start()

    for k in range(1, nt):
        sq_copy(k, t).start()

    @pl.when(first)
    def _():
        quarter.start(0, Q_PIECES)
        corr[...] = jnp.zeros_like(corr)

    @pl.when(odd_inner)
    def _():
        quarter_copy(0).wait_recv()
        quarter.start(0, Q_PIECES)

    @pl.when(odd)
    def _():
        quarter.start(Q_PIECES, 2 * Q_PIECES)

    @pl.when(hurried)
    def _():
        whole.start(PIECES // 2, PIECES)

    gain = gain_ref[...].astype(jnp.float32)
    for k in range(1, nt):
        sq_copy(k, t_peer(k)).wait_recv()
    total = squares[0]
    for j in range(1, nt):
        total = total + squares[j]
    scale = wide(lax.rsqrt(total / width + EPS), cols)
    x = x_ref[...].astype(jnp.float32) * scale
    xhat[...] = x
    normed_all[d] = (x * gain).astype(jnp.bfloat16)
    corr_own[...] = (x * scale).astype(jnp.bfloat16)
    upd[...] = scale

    @pl.when(odd)
    def _():
        for k in range(nt):
            corr_copy(k, True).start()

    @pl.when(even_inner)
    def _():
        corr_copy(0, False).start()

    def pass_turn():
        pl.semaphore_signal(turn, 1, device_id={"section": s - 1}, device_id_type=MESH)

    @pl.when(odd)
    def _():
        quarter.start(2 * Q_PIECES, quarter.steps)

        @pl.when(first)
        def _():
            for c in range(CHUNKS):
                for k in range(1, nt):
                    spread_copy(c, k, t).start()

        @pl.when(hurried)
        def _():
            whole.start(PIECES, 2 * PIECES)

        @pl.when(jnp.logical_and(odd_inner, jnp.logical_not(hurried)))
        def _():
            whole.start(0, PIECES)

        quarter.finish()
        for k in range(1, nt):
            gq_copy(k, t_peer(k)).wait_recv()
        back = jnp.zeros((tokens, cols), jnp.float32)
        for j in range(nt):
            back = back + jnp.dot(g_part[j], w_part[j], preferred_element_type=jnp.float32)

        @pl.when(first)
        def _():
            back_part[...] = back

        @pl.when(not_first)
        def _():
            back_sent[...] = back.astype(jnp.bfloat16)
            for c in range(CHUNKS):
                back_copy(c, plane).start()
            @pl.when(jnp.logical_not(hurried))
            def _():
                whole.start(PIECES, 2 * PIECES)

            corr_spread(1, t).wait_recv()
            for k in range(1, nt):
                corr_spread(k, t).start()
            whole.start(2 * PIECES, TURN)
            pass_turn()
            whole.start(TURN, whole.steps)
            whole.finish()

    @pl.when(even)
    def _():
        @pl.when(s < ns - 2)
        def _():
            pl.semaphore_wait(turn, 1)
            whole.start(0, PIECES)

        whole.start(PIECES, whole.steps)
        pl.semaphore_signal(free, 1, device_id={"section": s + 1}, device_id_type=MESH)
        whole.finish()

    @pl.when(early)
    def _():
        @pl.when(odd)
        def _():
            pl.semaphore_wait(free, 1)

        for k in range(1, nd):
            norm_copy(k, d).start()

    @pl.when(not_first)
    def _():
        @pl.when(even)
        def _():
            corr_spread(1, t).wait_recv()

        for k in range(1, nt):
            corr_spread(k, t_peer(k)).wait_recv()

    gain_part[d] = jnp.zeros((8, cols), jnp.float32)

    def pass_on(c):
        @pl.when(jnp.logical_and(odd_inner, c < CHUNKS))
        def _():
            spread_copy(c, 1, t).wait_recv()
            for k in range(1, nt):
                spread_copy(c, k, t).start()

    def chunk(c, carry):
        view = pl.ds(pl.multiple_of(c * rows, rows), rows)

        pass_on(c + AHEAD)

        @pl.when(even)
        def _():
            spread_copy(c, 1, t).wait_recv()

        for k in range(1, nt):
            spread_copy(c, k, t_peer(k)).wait_recv()
        r = inbox[0, view, cols:].astype(jnp.float32)
        for j in range(1, nt):
            r = r + inbox[j, view, cols:].astype(jnp.float32)
        r = wide(r, cols)
        for j in range(nt):
            g = inbox[j, view, :cols].astype(jnp.float32) - corr[j, view].astype(jnp.float32) * r
            grad_all[j, view] = g.astype(jnp.bfloat16)

        @pl.when(first)
        def _():
            back = back_part[view]
            for p in range(planes - 1):
                remote(
                    back_sent.at[view], back_in.at[p, view], back_send.at[c], back_recv.at[c, p],
                    {"section": 1},
                ).wait_recv()
                back = back + back_in[p, view].astype(jnp.float32)
            back_now[...] = back

        @pl.when(not_first)
        def _():
            back = jnp.zeros((rows, cols), jnp.float32)
            for j in range(nt):
                back = back + jnp.dot(
                    grad_all[j, view], w_all[j], preferred_element_type=jnp.float32
                )
            back_now[...] = back

        back = back_now[...]
        xh = xhat[view]
        weighted = gain * back
        part = jnp.sum(weighted * xh, axis=1, keepdims=True) * (1.0 / width)
        u = grad_all[t, view].astype(jnp.float32) + upd[view] * weighted
        outbox[view, :cols] = u.astype(jnp.bfloat16)
        tile = jnp.broadcast_to(part, (rows, LANES)).astype(jnp.bfloat16)
        outbox[view, cols:] = tile

        @pl.when(odd)
        def _():
            for k in range(nt):
                relay_copy(c, k, True).start()

        @pl.when(even_inner)
        def _():
            relay_copy(c, 0, False).start()

        @pl.when(jnp.logical_and(early, not_final))
        def _():
            for k in range(1, nd):
                swap_copy(c, k).start()
            swapped[d, view] = grad_all[d, view]

        @pl.when(final)
        def _():
            for k in range(1, nd):
                slice_copy(c, k).start()
            mine, lanes = slice_of(c)
            swapped[d, mine, lanes] = grad_all[d, mine, lanes]

        upd[view] = u
        rterm[t, view] = tile
        gain_part[d] = gain_part[d] + jnp.sum((back * xh).reshape(rows // 8, 8, cols), axis=0)
        return carry

    for c in range(AHEAD):
        pass_on(c)
    lax.fori_loop(0, CHUNKS, chunk, 0)

    def r_copy(k, src):
        return remote(rterm.at[src], rterm.at[src], r_send.at[k], r_recv.at[src], {"tensor": t_peer(k)})

    def gn_copy(k, src):
        return remote(
            gain_part.at[src], gain_part.at[src], gn_send.at[k], gn_recv.at[src], {"dp": dp_peer(k)}
        )

    for k in range(1, nt):
        r_copy(k, t).start()

    @pl.when(odd_late)
    def _():
        pl.semaphore_wait(free, 1)
        for k in range(1, nd):
            norm_copy(k, d).start()
            for c in range(CHUNKS):
                swap_copy(c, k).start()
        swapped[d] = grad_all[d]

    @pl.when(final)
    def _():
        for c in range(CHUNKS):
            mine, lanes = slice_of(c)
            for k in range(1, nd):
                src = dp_peer(k)
                remote(
                    grad_all.at[src, mine, lanes], swapped.at[src, mine, lanes],
                    swap_send.at[c, k], swap_recv.at[c, src], {"dp": dp_peer(1)},
                ).wait_recv()
            for k in range(1, nt):
                cross_copy(c, k).start()

    for k in range(1, nd):
        gn_copy(k, d).start()
    for k in range(1, nt):
        r_copy(k, t_peer(k)).wait_recv()
    r = rterm[0].astype(jnp.float32)
    for j in range(1, nt):
        r = r + rterm[j].astype(jnp.float32)
    grads_out[...] = (
        upd[...] - corr_own[...].astype(jnp.float32) * wide(r, cols)
    ).astype(jnp.bfloat16)
    for k in range(1, nd):
        gn_copy(k, dp_peer(k)).wait_recv()
    sums = gain_part[0]
    for j in range(1, nd):
        sums = sums + gain_part[j]
    gain_out[...] = jnp.sum(sums, axis=0, keepdims=True)

    for k in range(1, nd):
        norm_copy(k, dp_peer(k)).wait_recv()

    @pl.when(not_final)
    def _():
        for k in range(1, nd):
            src = dp_peer(k)
            for c in range(CHUNKS):
                view = pl.ds(c * rows, rows)
                remote(
                    grad_all.at[src, view], swapped.at[src, view], swap_send.at[c, k],
                    swap_recv.at[c, src], {"dp": dp_peer(1)},
                ).wait_recv()

    @pl.when(final)
    def _():
        groups = cols // LANES
        height = rows // (nt // groups)
        for k in range(1, nt):
            src = t_peer(k)
            lanes = pl.ds(pl.multiple_of(lax.rem(src, groups) * LANES, LANES), LANES)
            for c in range(CHUNKS):
                theirs = pl.ds(pl.multiple_of(c * rows + src // groups * height, height), height)
                view = swapped.at[:, theirs, lanes]
                remote(
                    view, view, cross_send.at[c, k], cross_recv.at[c, src], {"tensor": t_peer(1)}
                ).wait_recv()

    acc = jnp.zeros((cols, cols), jnp.float32)
    for j in range(nd):
        acc = acc + lax.dot_general(
            normed_all[j], swapped[j], (((0,), (0,)), ((), ())), preferred_element_type=jnp.float32
        )
    wgrad_out[...] = acc

    for k in range(1, nt):
        sq_copy(k, t).wait_send()
        r_copy(k, t).wait_send()
    for k in range(1, nd):
        norm_copy(k, d).wait_send()
        gn_copy(k, d).wait_send()

    @pl.when(not_final)
    def _():
        for k in range(1, nd):
            for c in range(CHUNKS):
                swap_copy(c, k).wait_send()

    @pl.when(final)
    def _():
        for c in range(CHUNKS):
            for k in range(1, nd):
                slice_copy(c, k).wait_send()
            for k in range(1, nt):
                cross_copy(c, k).wait_send()

    @pl.when(not_first)
    def _():
        whole.drain()

    @pl.when(odd)
    def _():
        quarter.drain()
        for k in range(1, nt):
            gq_copy(k, t).wait_send()
            for c in range(CHUNKS):
                spread_copy(c, k, t).wait_send()
        for k in range(nt):
            for c in range(CHUNKS):
                relay_copy(c, k, True).wait_send()

    @pl.when(odd_inner)
    def _():
        for c in range(CHUNKS):
            back_copy(c, plane).wait_send()

    @pl.when(first)
    def _():
        for p in range(planes - 1):
            quarter_copy(p).wait_send()

    @pl.when(odd)
    def _():
        for k in range(nt):
            corr_copy(k, True).wait_send()

    @pl.when(odd_inner)
    def _():
        for k in range(1, nt):
            corr_spread(k, t).wait_send()

    @pl.when(even_inner)
    def _():
        corr_copy(0, False).wait_send()
        for c in range(CHUNKS):
            relay_copy(c, 0, False).wait_send()


def per_device(activations, cotangent, lengths, weights, gains):
    ns, nt, nd = (lax.axis_size(a) for a in ("section", "tensor", "dp"))
    _, micro, seqlen, cols = activations.shape
    tokens = micro * seqlen
    planes = ns // 2
    bf16, f32 = jnp.bfloat16, jnp.float32
    vmem = pl.BlockSpec(memory_space=pltpu.VMEM)
    hbm = pl.BlockSpec(memory_space=pl.ANY)
    dma = lambda *shape: pltpu.SemaphoreType.DMA(shape)
    ring = lambda pieces: dma(2, nd // 2, pieces)
    grads, wgrad, gain_grad = pl.pallas_call(
        functools.partial(kernel, (ns, nt, nd)),
        out_shape=(
            jax.ShapeDtypeStruct((tokens, cols), bf16),
            jax.ShapeDtypeStruct((cols, cols), f32),
            jax.ShapeDtypeStruct((1, cols), f32),
        ),
        in_specs=[pl.BlockSpec(memory_space=pltpu.SMEM)] + [hbm] * 4,
        out_specs=(vmem, vmem, vmem),
        scratch_shapes=[
            pltpu.VMEM((tokens, cols), bf16),
            pltpu.VMEM((tokens, cols), bf16),
            pltpu.VMEM((cols, cols), bf16),
            pltpu.VMEM((1, cols), bf16),
            pltpu.VMEM((nd, cols, cols), bf16),
            pltpu.VMEM((nt, tokens, cols + LANES), bf16),
            pltpu.VMEM((nt, tokens, cols), bf16),
            pltpu.VMEM((nt, tokens, cols), bf16),
            pltpu.VMEM((tokens, cols), bf16),
            pltpu.VMEM((nd, tokens, cols), bf16),
            pltpu.VMEM((nd, tokens, cols), bf16),
            pltpu.VMEM((tokens, cols), f32),
            pltpu.VMEM((tokens, cols), f32),
            pltpu.VMEM((tokens, cols + LANES), bf16),
            pltpu.VMEM((nt, tokens, LANES), f32),
            pltpu.VMEM((nt, tokens, LANES), bf16),
            pltpu.VMEM((nd, 8, cols), f32),
            pltpu.VMEM((nd, cols // planes, cols), bf16),
            pltpu.VMEM((nt, tokens, cols // planes), bf16),
            pltpu.VMEM((tokens, cols), f32),
            pltpu.VMEM((tokens, cols), bf16),
            pltpu.VMEM((planes - 1, tokens, cols), bf16),
            pltpu.VMEM((tokens // CHUNKS, cols), f32),
            dma(4),
            ring(PIECES), ring(PIECES), ring(Q_PIECES), ring(Q_PIECES),
            dma(CHUNKS, nt), dma(CHUNKS, nt),
            dma(CHUNKS, nd), dma(CHUNKS, nd),
            dma(nt), dma(nt), dma(nt), dma(nt), dma(nd), dma(nd),
            dma(nt), dma(nt), dma(nd), dma(nd),
            dma(planes), pltpu.SemaphoreType.DMA, dma(nt), dma(nt),
            dma(CHUNKS), dma(CHUNKS, planes), dma(CHUNKS, nt), dma(nt),
            dma(CHUNKS, nt), dma(CHUNKS, nt),
            pltpu.SemaphoreType.REGULAR, pltpu.SemaphoreType.REGULAR,
        ],
        compiler_params=pltpu.CompilerParams(
            collective_id=0, has_side_effects=True, vmem_limit_bytes=56 << 20
        ),
        name="relay",
    )(
        lengths,
        activations.reshape(tokens, cols),
        cotangent.reshape(tokens, cols),
        weights.reshape(cols, cols),
        gains,
    )
    return (
        grads.reshape(1, micro, seqlen, cols),
        wgrad.reshape(1, cols, cols),
        gain_grad,
    )


def solution(mesh):
    in_specs = (
        P("section", "dp", None, "tensor"),
        P("dp", None, "tensor"),
        P("dp"),
        P("section", "tensor", "dp"),
        P("section", "tensor"),
    )
    out_specs = (
        P("section", "dp", None, "tensor"),
        P("section", "tensor", "dp"),
        P("section", "tensor"),
    )
    return jax.shard_map(
        per_device, mesh=mesh, in_specs=in_specs, out_specs=out_specs, check_vma=False
    )
```

time: 174 us -> 135 us (0.78)
  Pallas kernels: 166 us -> 130 us
    pallas_call x1, Pallas kernels: 166 us -> 130 us  [per_device(): pl.pallas_call(functools.partial(kernel, (ns, nt, nd)), out_shape=(jax.Sh...]
    unnamed x13 -> x5, local copies, waits for them, and re-layouts: 5.72 us -> 4.41 us
where the time goes in v2:
time: 135 us
  Pallas kernels  130 us (96%)
  local copies, waits for them, and re-layouts  4.41 us (3%)
    pallas_call x1, Pallas kernels, per_device(): pl.pallas_call(functools.partial(kernel, (ns, nt, nd)), out_shape=(jax.Sh...  130 us
    unnamed x5, local copies, waits for them, and re-layouts  4.41 us

profile of v2, /device:TPU:56, one launch (start us, length us, event | category | flops | bytes accessed | tf_op | source)
XLA Modules:
  0.0 135.0 jit_solution(10842859663102364765)
XLA Ops:
  0.6 129.9 %relay.1 = (bf16[128,512]{1,0:T(8,128)(2,1)}, f32[512,512]{1,0:T(8,128)}, f32[1,512]{1,0:T(1,128)}) custom-call(s32[2]{0:T(128)} %lengths_ref.1, bf16[128,512]{1,0:T(8,128)(2,1)} %bitcast.8, bf16[128,512]{1,0:T(8,128)(2,1)} %bitcast.9, bf16[512,512]{1,0:T(8,128)(2,1)} %bitcast.6, bf16[1,512]{1,0:T(2,128)(2,1)} %gain_hbm.1), custom_call_target="tpu_custom_call" | custom-call | tf_op jit(solution)/shard_map/relay/pallas_call | solution.py:660
  130.5 1.6 %copy.11 = bf16[1,2,64,512]{3,2,1,0:T(8,128)(2,1)} copy(bf16[1,2,64,512]{3,2,1,0:T(8,128)(2,1)} %bitcast.7) | data formatting | bytes 262144
  132.1 0.0 copy-start
  132.1 2.3 %copy.12 = f32[1,512,512]{2,1,0:T(8,128)} copy(f32[1,512,512]{2,1,0:T(8,128)} %bitcast.5) | data formatting | bytes 2097152
  134.4 0.0 copy-done
  134.4 0.6 copy.13
Async XLA Ops:
  132.1 2.3 %copy-start = (f32[1,512]{1,0:T(1,128)S(1)}, f32[1,512]{1,0:T(1,128)}, u32[]{:S(2)}) copy-start(f32[1,512]{1,0:T(1,128)} %get-tuple-element.14) | copy-start | bytes 6148

commit v3 on v2

--- a/solution.py
+++ b/solution.py
@@ -13,7 +13,7 @@
 WINDOW = 2
 Q_PIECES = 2
 TURN = 8
-FINAL = 1
+SPLIT = 2
 AHEAD = 2
 PIECES = 4
 MESH = pl.DeviceIdType.MESH
@@ -107,8 +107,7 @@
     even_inner = jnp.logical_and(even, not_last)
     odd_late = jnp.logical_and(odd, s >= ns // 2)
     hurried = s == ns - 3
-    final = s < FINAL
-    not_final = jnp.logical_not(final)
+    staged = lambda c: jnp.logical_or(last, jnp.logical_and(s == 1, c >= SPLIT))
     early = jnp.logical_not(odd_late)
     dp_peer = lambda k: lax.rem(d + k, nd)
     t_peer = lambda k: lax.rem(t + k, nt)
@@ -477,13 +476,13 @@
         def _():
             relay_copy(c, 0, False).start()
 
-        @pl.when(jnp.logical_and(early, not_final))
+        @pl.when(jnp.logical_and(early, jnp.logical_not(staged(c))))
         def _():
             for k in range(1, nd):
                 swap_copy(c, k).start()
             swapped[d, view] = grad_all[d, view]
 
-        @pl.when(final)
+        @pl.when(staged(c))
         def _():
             for k in range(1, nd):
                 slice_copy(c, k).start()
@@ -519,9 +518,10 @@
                 swap_copy(c, k).start()
         swapped[d] = grad_all[d]
 
-    @pl.when(final)
-    def _():
-        for c in range(CHUNKS):
+    for c in range(CHUNKS):
+
+        @pl.when(staged(c))
+        def _():
             mine, lanes = slice_of(c)
             for k in range(1, nd):
                 src = dp_peer(k)
@@ -552,25 +552,25 @@
     for k in range(1, nd):
         norm_copy(k, dp_peer(k)).wait_recv()
 
-    @pl.when(not_final)
-    def _():
-        for k in range(1, nd):
-            src = dp_peer(k)
-            for c in range(CHUNKS):
+    groups = cols // LANES
+    height = rows // (nt // groups)
+    for c in range(CHUNKS):
+
+        @pl.when(jnp.logical_not(staged(c)))
+        def _():
+            for k in range(1, nd):
+                src = dp_peer(k)
                 view = pl.ds(c * rows, rows)
                 remote(
                     grad_all.at[src, view], swapped.at[src, view], swap_send.at[c, k],
                     swap_recv.at[c, src], {"dp": dp_peer(1)},
                 ).wait_recv()
 
-    @pl.when(final)
-    def _():
-        groups = cols // LANES
-        height = rows // (nt // groups)
-        for k in range(1, nt):
-            src = t_peer(k)
-            lanes = pl.ds(pl.multiple_of(lax.rem(src, groups) * LANES, LANES), LANES)
-            for c in range(CHUNKS):
+        @pl.when(staged(c))
+        def _():
+            for k in range(1, nt):
+                src = t_peer(k)
+                lanes = pl.ds(pl.multiple_of(lax.rem(src, groups) * LANES, LANES), LANES)
                 theirs = pl.ds(pl.multiple_of(c * rows + src // groups * height, height), height)
                 view = swapped.at[:, theirs, lanes]
                 remote(
@@ -591,15 +591,15 @@
         norm_copy(k, d).wait_send()
         gn_copy(k, d).wait_send()
 
-    @pl.when(not_final)
-    def _():
-        for k in range(1, nd):
-            for c in range(CHUNKS):
+    for c in range(CHUNKS):
+
+        @pl.when(jnp.logical_not(staged(c)))
+        def _():
+            for k in range(1, nd):
                 swap_copy(c, k).wait_send()
 
-    @pl.when(final)
-    def _():
-        for c in range(CHUNKS):
+        @pl.when(staged(c))
+        def _():
             for k in range(1, nd):
                 slice_copy(c, k).wait_send()
             for k in range(1, nt):
@@ -645,6 +645,12 @@
         corr_copy(0, False).wait_send()
         for c in range(CHUNKS):
             relay_copy(c, 0, False).wait_send()
+
+
+def copy_out(a, b, c, a_out, b_out, c_out):
+    a_out[...] = a[...]
+    b_out[...] = b[...]
+    c_out[...] = c[...]
 
 
 def per_device(activations, cotangent, lengths, weights, gains):
@@ -712,6 +718,26 @@
         weights.reshape(cols, cols),
         gains,
     )
+    grads, wgrad, gain_grad = pl.pallas_call(
+        copy_out,
+        out_shape=(
+            jax.ShapeDtypeStruct((tokens, cols), bf16),
+            jax.ShapeDtypeStruct((cols, cols), f32),
+            jax.ShapeDtypeStruct((1, cols), f32),
+        ),
+        grid=(4,),
+        in_specs=[
+            pl.BlockSpec((tokens // 4, cols), lambda i: (i, 0)),
+            pl.BlockSpec((cols // 4, cols), lambda i: (i, 0)),
+            pl.BlockSpec((1, cols), lambda i: (0, 0)),
+        ],
+        out_specs=(
+            pl.BlockSpec((tokens // 4, cols), lambda i: (i, 0)),
+            pl.BlockSpec((cols // 4, cols), lambda i: (i, 0)),
+            pl.BlockSpec((1, cols), lambda i: (0, 0)),
+        ),
+        name="copy_out",
+    )(grads, wgrad, gain_grad)
     return (
         grads.reshape(1, micro, seqlen, cols),
         wgrad.reshape(1, cols, cols),

time: 135 us -> 134 us (level)
  local copies, waits for them, and re-layouts: 4.41 us -> 0 us
  Pallas kernels: 130 us -> 133 us
    unnamed x5 -> x0, local copies, waits for them, and re-layouts: 4.41 us -> none
    pallas_call x0 -> x1, Pallas kernels: none -> 3.45 us  [per_device(): pl.pallas_call(copy_out, out_shape=(jax.ShapeDtypeStruct((tokens, cols),...]
where the time goes in v3:
time: 134 us
  Pallas kernels  133 us (99%)
    pallas_call x1, Pallas kernels, per_device(): pl.pallas_call(functools.partial(kernel, (ns, nt, nd)), out_shape=(jax.Sh...  130 us
    pallas_call x1, Pallas kernels, per_device(): pl.pallas_call(copy_out, out_shape=(jax.ShapeDtypeStruct((tokens, cols),...  3.45 us

profile of v3, /device:TPU:56, one launch (start us, length us, event | category | flops | bytes accessed | tf_op | source)
XLA Modules:
  0.0 133.8 jit_solution(3169115207500815847)
XLA Ops:
  0.6 129.7 %relay.1 = (bf16[128,512]{1,0:T(8,128)(2,1)}, f32[512,512]{1,0:T(8,128)}, f32[1,512]{1,0:T(1,128)}) custom-call(s32[2]{0:T(128)} %lengths_ref.1, bf16[128,512]{1,0:T(8,128)(2,1)} %bitcast.6, bf16[128,512]{1,0:T(8,128)(2,1)} %bitcast.7, bf16[512,512]{1,0:T(8,128)(2,1)} %bitcast.5, bf16[1,512]{1,0:T(2,128)(2,1)} %gain_hbm.1), custom_call_target="tpu_custom_call" | custom-call | tf_op jit(solution)/shard_map/relay/pallas_call | solution.py:666
  130.3 3.4 %copy_out.1 = (bf16[128,512]{1,0:T(8,128)(2,1)}, f32[512,512]{1,0:T(8,128)}, f32[1,512]{1,0:T(1,128)}) custom-call(bf16[128,512]{1,0:T(8,128)(2,1)} %get-tuple-element.9.a, f32[512,512]{1,0:T(8,128)} %get-tuple-element.10.b, f32[1,512]{1,0:T(1,128)} %get-tuple-element.11.c), custom_call_target="tpu_custom_call" | custom-call | tf_op jit(solution)/shard_map/copy_out/pallas_call | solution.py:721
